TPU v7x, 256 devices: a whole 4x4x8 slice. The times are simulated.
256 devices in a mesh: expert: 16 (over x_lo, y, core), hidden: 16 (over z, x_hi).
Axes of the slice: x: 4 (x_hi: 2, x_lo: 2; x = x_hi * 2 + x_lo), y: 4, z: 8, core: 2. Of those that a mesh axis runs over, the one named last changes fastest.
Arguments:
- tokens: bfloat16 [4096, 7168], P('expert', 'hidden'), may hold values from -6 to 6
- route_ids: int32 [4096, 2], P('expert'), may hold values from 0 to 15, all different within a row; in each aligned block of 256 rows (0 to 255, 256 to 511, ...) at most 40 rows name the same one
- route_weight: float32 [4096, 2], P('expert'), may hold values from 0.2 to 2
- w_gate: bfloat16 [16, 7168, 2048], P('expert', None, 'hidden'), may hold values from -0.0625 to 0.0625
- w_up: bfloat16 [16, 7168, 2048], P('expert', None, 'hidden'), may hold values from -0.0625 to 0.0625
- w_down: bfloat16 [16, 2048, 7168], P('expert', 'hidden'), may hold values from -0.125 to 0.125
Outputs:
- mixed: bfloat16 [4096, 7168], P('expert', 'hidden')
Inputs may be any that keep to these rules, and one draw needn't show every extreme that they name: `route_ids`: each row names 2 different experts. In the aligned blocks of 256 rows, no expert is named by more than 40 rows of one block, a bound that some block reaches.
All inputs are finite; a program needn't handle non-finite values.
Results may differ from a plain program's by a relative error of at most 0.0057.
Values may be sent and summed in bfloat16 or wider, within the bound.
No kernel may reach another device: no remote copies, remote signals or barrier semaphores. Data moves between devices by JAX's collectives and lax.ppermute only.
A program may use at most 128 MiB of HBM per device.

v0:
```python
import jax
import jax.numpy as jnp
from jax import lax
from jax.sharding import PartitionSpec as P

TOP = 2


def on_device(tokens, route_ids, route_weight, w_gate, w_up, w_down):
    experts = lax.axis_size("expert")
    parts = lax.axis_size("hidden")
    rows_dev, width = tokens.shape
    capacity = (rows_dev * TOP * 5 + 4 * experts - 1) // (4 * experts)
    slot_count = experts * capacity
    matches = route_ids[:, :, None] == jnp.arange(experts, dtype=jnp.int32)[None, None, :]
    chosen = jnp.any(matches, axis=1)
    before = jnp.arange(rows_dev)[:, None] > jnp.arange(rows_dev)[None, :]
    ranking = jnp.dot(
        before.astype(jnp.bfloat16), chosen.astype(jnp.bfloat16), preferred_element_type=jnp.float32
    )
    slot_of = jnp.arange(experts, dtype=jnp.float32)[None, :] * capacity + ranking
    slot_k = jnp.sum(jnp.where(matches, slot_of[:, None, :], 0.0), axis=2).astype(jnp.int32)
    slots = jnp.arange(slot_count, dtype=jnp.int32)
    picks_k = [slot_k[:, k][:, None] == slots[None, :] for k in range(TOP)]
    picks = (picks_k[0] | picks_k[1]).astype(jnp.bfloat16)
    down_w = lax.all_to_all(w_down[0], "hidden", split_axis=1, concat_axis=0, tiled=True)
    leaving = lax.dot_general(
        picks, tokens, (((0,), (0,)), ((), ())), preferred_element_type=jnp.float32
    ).astype(jnp.bfloat16)
    arrived = lax.all_to_all(
        leaving.reshape(experts, capacity, width), "expert", split_axis=0, concat_axis=0, tiled=True
    ).reshape(slot_count, width)
    rows = lax.all_gather(arrived, "hidden", axis=1, tiled=True)
    gate_sum = jnp.dot(rows, w_gate[0], preferred_element_type=jnp.float32)
    up_sum = jnp.dot(rows, w_up[0], preferred_element_type=jnp.float32)
    hidden = (jax.nn.silu(gate_sum) * up_sum).astype(jnp.bfloat16)
    every_hidden = lax.all_gather(hidden, "hidden", axis=1, tiled=True)
    produced = jnp.dot(every_hidden, down_w, preferred_element_type=jnp.float32).astype(
        jnp.bfloat16
    )
    returned = lax.all_to_all(
        produced.reshape(experts, capacity, width),
        "expert",
        split_axis=0,
        concat_axis=0,
        tiled=True,
    ).reshape(slot_count, width)
    mixed = jnp.zeros((rows_dev, width), jnp.float32)
    for k in range(TOP):
        result = jnp.dot(
            picks_k[k].astype(jnp.bfloat16), returned, preferred_element_type=jnp.float32
        )
        mixed = mixed + route_weight[:, k][:, None] * result
    return mixed.astype(jnp.bfloat16)


def solution(mesh):
    in_specs = (
        P("expert", "hidden"),
        P("expert", None),
        P("expert", None),
        P("expert", None, "hidden"),
        P("expert", None, "hidden"),
        P("expert", "hidden", None),
    )
    out_specs = P("expert", "hidden")
    return jax.shard_map(
        on_device, mesh=mesh, in_specs=in_specs, out_specs=out_specs, check_vma=False
    )
```

profile of v0, /device:TPU:1, one launch (start us, length us, event | category | flops | bytes accessed | tf_op | source)
XLA Modules:
  0.0 319.6 jit_solution(8556425088492365411)
XLA Ops:
  6.5 0.0 copy-start
  6.5 0.0 all-gather.3.cloned.1.call-start
  6.5 0.8 fusion.24
  7.4 0.2 convolution_add_fusion
  7.5 0.7 select_reduce_fusion
  8.3 1.5 convolution_convert_fusion
  9.8 0.3 copy.22
  10.1 18.5 %all_to_all.29 = bf16[16,40,448]{2,1,0:T(8,128)(2,1)S(1)} all-to-all(bf16[16,40,448]{2,1,0:T(8,128)(2,1)S(1)} %bitcast.39), channel_id=1, replica_groups=mesh['expert'=16,'hidden'=16] {'expert'}, dimensions={0} | all-to-all | bytes 1146880 | tf_op jit(solution)/shard_map/all_to_all | solution.py:30
  28.5 1.1 copy.23
  29.6 0.0 all-gather.3.cloned.1.call-update
  29.6 0.0 all-gather.5.cloned.1.call-start
  29.7 143.9 %all-gather.3.cloned.1.call-done = bf16[640,7168]{0,1:T(8,128)(2,1)} async-done(((bf16[640,448]{0,1:T(8,128)(2,1)}), bf16[640,7168]{0,1:T(8,128)(2,1)}) %all-gather.3.cloned.1.call-update) | async-done | bytes 9175056 | tf_op jit(solution)/shard_map/all_gather | solution.py:33
  173.6 0.0 copy-done
  173.6 0.0 copy-start.2
  173.6 0.0 copy-start.3
  173.6 6.3 %fusion.5 = f32[640,128]{1,0:T(8,128)S(1)} fusion(bf16[640,7168]{0,1:T(8,128)(2,1)} %all-gather.3.cloned.1.call-done, bf16[1,7168,128]{2,1,0:T(8,128)(2,1)S(1)} %copy-done), kind=kOutput, calls=%fused_computation.5 | convolution fusion | flops 1174405120 | bytes 11337728 | tf_op jit(solution)/shard_map/dot_general | solution.py:34
  179.9 0.0 copy-done.2
  179.9 0.4 copy-done.3
  180.3 3.2 %fusion.15 = bf16[640,128]{1,0:T(8,128)(2,1)} fusion(bf16[640,7168]{0,1:T(8,128)(2,1)S(1)} %copy-done.2, bf16[1,7168,128]{2,1,0:T(8,128)(2,1)S(1)} %copy-done.3, f32[640,128]{1,0:T(8,128)S(1)} %fusion.5), kind=kOutput, calls=%fused_computation.14 | convolution fusion | flops 1174896640 | bytes 11501568 | tf_op jit(solution)/shard_map/dot_general | solution.py:35
  183.6 0.0 all-gather.5.cloned.1.call-update
  183.6 3.9 %copy.24 = bf16[1,128,7168]{1,2,0:T(8,128)(2,1)} copy(bf16[1,128,7168]{2,1,0:T(8,128)(2,1)} %param.11) | data formatting | bytes 3670016 | tf_op args[5]
  187.5 56.4 %all_to_all.30 = bf16[128,16,448]{0,2,1:T(8,128)(2,1)} all-to-all(bf16[128,16,448]{0,2,1:T(8,128)(2,1)} %bitcast.36), channel_id=1, replica_groups=mesh['expert'=16,'hidden'=16] {'hidden'}, dimensions={1} | all-to-all | bytes 3670016 | tf_op jit(solution)/shard_map/all_to_all | solution.py:26
  243.9 42.7 %all-gather.5.cloned.1.call-done = bf16[640,2048]{1,0:T(8,128)(2,1)} async-done(((bf16[640,128]{1,0:T(8,128)(2,1)}), bf16[640,2048]{1,0:T(8,128)(2,1)}) %all-gather.5.cloned.1.call-update) | async-done | bytes 2621456 | tf_op jit(solution)/shard_map/all_gather | solution.py:37
  286.5 3.9 %fusion.7 = bf16[640,448]{0,1:T(8,128)(2,1)S(1)} fusion(bf16[640,2048]{1,0:T(8,128)(2,1)} %all-gather.5.cloned.1.call-done, bf16[128,16,448]{0,2,1:T(8,128)(2,1)} %all_to_all.30), kind=kOutput, calls=%fused_computation.7 | convolution fusion | flops 1174691840 | bytes 5029888 | tf_op jit(solution)/shard_map/dot_general | solution.py:38
  290.4 0.0 copy-start.1
  290.4 1.1 copy.26
  291.5 8.3 %all-to-all-start.2 = ((bf16[16,40,448]{2,1,0:T(8,128)(2,1)}), bf16[16,40,448]{2,1,0:T(8,128)(2,1)S(1)}, u32[]{:S(2)}, u32[]{:S(2)}) async-start(bf16[16,40,448]{2,1,0:T(8,128)(2,1)} %bitcast.9), calls=%async_computation.2 | async-start | bytes 1310720 | tf_op jit(solution)/shard_map/all_to_all | solution.py:41
  299.8 0.0 copy-done.1
  299.8 11.2 %all-to-all-done.2 = bf16[16,40,448]{2,1,0:T(8,128)(2,1)S(1)} async-done(((bf16[16,40,448]{2,1,0:T(8,128)(2,1)}), bf16[16,40,448]{2,1,0:T(8,128)(2,1)S(1)}, u32[]{:S(2)}, u32[]{:S(2)}) %all-to-all-start.2) | async-done | bytes 573472 | tf_op jit(solution)/shard_map/all_to_all | solution.py:41
  311.1 0.5 convolution_multiply_fusion.1
  311.5 1.2 fusion.11
  (4 shorter events, 0.0 us)
Async XLA Ops:
  6.5 167.0 %copy-start = (bf16[1,7168,128]{2,1,0:T(8,128)(2,1)S(1)}, bf16[1,7168,128]{2,1,0:T(8,128)(2,1)}, u32[]{:S(2)}) copy-start(bf16[1,7168,128]{2,1,0:T(8,128)(2,1)} %param.9) | copy-start | bytes 5505028
  6.5 167.0 %all-gather.3.cloned.1.call-start = ((), (), s32[]{:S(2)}) async-start(), calls=%async_computation.3 | async-start | bytes 9748480 | tf_op jit(solution)/shard_map/all_gather | solution.py:33
  29.6 256.9 %all-gather.5.cloned.1.call-start = ((), (), s32[]{:S(2)}) async-start(), calls=%async_computation.4 | async-start | bytes 2785280 | tf_op jit(solution)/shard_map/all_gather | solution.py:37
  173.6 6.3 %copy-start.2 = (bf16[640,7168]{0,1:T(8,128)(2,1)S(1)}, bf16[640,7168]{0,1:T(8,128)(2,1)}, u32[]{:S(2)}) copy-start(bf16[640,7168]{0,1:T(8,128)(2,1)} %all-gather.3.cloned.1.call-done) | copy-start | bytes 27525124
  173.6 6.7 %copy-start.3 = (bf16[1,7168,128]{2,1,0:T(8,128)(2,1)S(1)}, bf16[1,7168,128]{2,1,0:T(8,128)(2,1)}, u32[]{:S(2)}) copy-start(bf16[1,7168,128]{2,1,0:T(8,128)(2,1)} %param.10) | copy-start | bytes 5505028
  290.4 9.4 %copy-start.1 = (f32[256,2]{0,1:T(2,128)S(1)}, f32[256,2]{0,1:T(2,128)}, u32[]{:S(2)}) copy-start(f32[256,2]{0,1:T(2,128)} %param.8) | copy-start | bytes 6148
  291.5 19.5 %all-to-all-start.2 = ((bf16[16,40,448]{2,1,0:T(8,128)(2,1)}), bf16[16,40,448]{2,1,0:T(8,128)(2,1)S(1)}, u32[]{:S(2)}, u32[]{:S(2)}) async-start(bf16[16,40,448]{2,1,0:T(8,128)(2,1)} %bitcast.9), calls=%async_computation.2 | async-start | bytes 1310720 | tf_op jit(solution)/shard_map/all_to_all | solution.py:41
Sparse Core Ops, SparseCore 0:
  29.7 143.7 all-gather.2
  183.7 102.7 all-gather.4
where the time goes:
time: 320 us
  waiting for transfers between devices  198 us (62%)
  blocking collectives  74.9 us (23%)
  matrix products  16.8 us (5%)
  between operations  13.5 us (4%)
  starting transfers between devices  8.31 us (3%)
  local copies, waits for them, and re-layouts  6.73 us (2%)
    all_gather x1, waiting for transfers between devices, on_device(): rows = lax.all_gather(arrived, 'hidden', axis=1, tiled=True)  144 us
    all_to_all x1, blocking collectives, on_device(): lax.all_to_all(w_down[0], 'hidden', split_axis=1, concat_axis=0, tiled=True)  56.4 us
    all_gather x1, waiting for transfers between devices, on_device(): every_hidden = lax.all_gather(hidden, 'hidden', axis=1, tiled=True)  42.7 us
    all_to_all x1, blocking collectives, on_device(): lax.all_to_all(leaving.reshape(experts, capacity, width), 'expert', split...  18.5 us
    all_to_all x1, waiting for transfers between devices, on_device(): lax.all_to_all(produced.reshape(experts, capacity, width), 'expert', spli...  11.2 us
    all_to_all x1, starting transfers between devices, on_device(): lax.all_to_all(produced.reshape(experts, capacity, width), 'expert', spli...  8.26 us
  transfers between devices with their start and end apart: 3, of which 3 were waited for; matrix products, arithmetic and copies ran while one was open for 1% of the time, Pallas kernels for 0%

commit v1 on v0

--- a/solution.py
+++ b/solution.py
@@ -23,7 +23,12 @@
     slots = jnp.arange(slot_count, dtype=jnp.int32)
     picks_k = [slot_k[:, k][:, None] == slots[None, :] for k in range(TOP)]
     picks = (picks_k[0] | picks_k[1]).astype(jnp.bfloat16)
-    down_w = lax.all_to_all(w_down[0], "hidden", split_axis=1, concat_axis=0, tiled=True)
+    down_w = jnp.concatenate(
+        lax.all_to_all(
+            jnp.stack(jnp.split(w_down[0], lax.axis_size("hidden"), axis=1), axis=0), "hidden", 0, 0
+        ),
+        axis=0,
+    )
     leaving = lax.dot_general(
         picks, tokens, (((0,), (0,)), ((), ())), preferred_element_type=jnp.float32
     ).astype(jnp.bfloat16)

time: 320 us -> 320 us (level)
  local copies, waits for them, and re-layouts: 6.73 us -> 31.6 us
  waiting for transfers between devices: 198 us -> 174 us
    unnamed x9 -> x24, local copies, waits for them, and re-layouts: 4.29 us -> 27.5 us
    all_gather x1, waiting for transfers between devices: 144 us -> 126 us  [on_device(): rows = lax.all_gather(arrived, 'hidden', axis=1, tiled=True)]
    all_gather x1, waiting for transfers between devices: 42.7 us -> 37.1 us  [on_device(): every_hidden = lax.all_gather(hidden, 'hidden', axis=1, tiled=True)]
  transfers between devices with their start and end apart: 3 -> 3, of which waited for: 3 -> 3; matrix products, arithmetic and copies ran while one was open for 1% -> 9% of each run, Pallas kernels for 0% -> 0%
where the time goes in v1:
time: 320 us; the launch traced here: 319 us
  waiting for transfers between devices  174 us (54%)
  blocking collectives  73.2 us (23%)
  local copies, waits for them, and re-layouts  31.6 us (10%)
  matrix products  16.8 us (5%)
  between operations  13.5 us (4%)
  starting transfers between devices  8.31 us (3%)
    all_gather x1, waiting for transfers between devices, on_device(): rows = lax.all_gather(arrived, 'hidden', axis=1, tiled=True)  126 us
    all_to_all x1, blocking collectives, on_device(): lax.all_to_all(jnp.stack(jnp.split(w_down[0], lax.axis_size('hidden'), ax...  54.7 us
    all_gather x1, waiting for transfers between devices, on_device(): every_hidden = lax.all_gather(hidden, 'hidden', axis=1, tiled=True)  37.1 us
    unnamed x24, local copies, waits for them, and re-layouts  27.5 us
    all_to_all x1, blocking collectives, on_device(): lax.all_to_all(leaving.reshape(experts, capacity, width), 'expert', split...  18.5 us
    all_to_all x1, waiting for transfers between devices, on_device(): lax.all_to_all(produced.reshape(experts, capacity, width), 'expert', spli...  11.2 us
    all_to_all x1, starting transfers between devices, on_device(): lax.all_to_all(produced.reshape(experts, capacity, width), 'expert', spli...  8.27 us
  transfers between devices with their start and end apart: 3, of which 3 were waited for; matrix products, arithmetic and copies ran while one was open for 9% of the time, Pallas kernels for 0%

profile of v1, /device:TPU:1, one launch (start us, length us, event | category | flops | bytes accessed | tf_op | source)
XLA Modules:
  0.0 319.3 jit_solution(10954217773843135116)
XLA Ops:
  6.5 0.8 fusion.40
  7.5 0.7 select_reduce_fusion
  8.3 1.5 convolution_convert_fusion
  10.1 18.5 %all_to_all.15 = bf16[16,40,448]{2,1,0:T(8,128)(2,1)S(1)} all-to-all(bf16[16,40,448]{2,1,0:T(8,128)(2,1)S(1)} %bitcast.117), channel_id=1, replica_groups=mesh['expert'=16,'hidden'=16] {'expert'}, dimensions={0} | all-to-all | bytes 1146880 | tf_op jit(solution)/shard_map/all_to_all | solution.py:35
  28.5 1.1 copy.27
  29.7 3.9 %copy.28 = bf16[1,128,7168]{1,2,0:T(8,128)(2,1)} copy(bf16[1,128,7168]{2,1,0:T(8,128)(2,1)} %param.11) | data formatting | bytes 3670016 | tf_op args[5]
  33.6 1.6 fusion.39
  35.2 1.5 fusion.38
  36.7 1.6 fusion.37
  38.3 1.6 fusion.36
  39.8 1.5 fusion.35
  41.4 1.6 fusion.34
  42.9 1.6 fusion.33
  44.5 1.5 fusion.32
  46.0 1.5 fusion.31
  47.6 126.1 %all-gather.3.cloned.1.call-done = bf16[640,7168]{0,1:T(8,128)(2,1)} async-done(((bf16[640,448]{0,1:T(8,128)(2,1)}), bf16[640,7168]{0,1:T(8,128)(2,1)}) %all-gather.3.cloned.1.call-update) | async-done | bytes 9175056 | tf_op jit(solution)/shard_map/all_gather | solution.py:38
  173.6 6.3 %fusion.5 = f32[640,128]{1,0:T(8,128)S(1)} fusion(bf16[640,7168]{0,1:T(8,128)(2,1)} %all-gather.3.cloned.1.call-done, bf16[1,7168,128]{2,1,0:T(8,128)(2,1)S(1)} %copy-done), kind=kOutput, calls=%fused_computation.5 | convolution fusion | flops 1174405120 | bytes 11337728 | tf_op jit(solution)/shard_map/dot_general | solution.py:39
  180.3 3.2 %fusion.15 = bf16[640,128]{1,0:T(8,128)(2,1)} fusion(bf16[640,7168]{0,1:T(8,128)(2,1)S(1)} %copy-done.2, bf16[1,7168,128]{2,1,0:T(8,128)(2,1)S(1)} %copy-done.3, f32[640,128]{1,0:T(8,128)S(1)} %fusion.5), kind=kOutput, calls=%fused_computation.14 | convolution fusion | flops 1174896640 | bytes 11501568 | tf_op jit(solution)/shard_map/dot_general | solution.py:40
  183.6 1.5 fusion.30
  185.2 1.6 fusion.29
  186.7 1.6 fusion.28
  188.3 1.5 fusion.27
  189.8 1.6 fusion.26
  191.4 1.5 fusion.25
  192.9 1.6 fusion.24
  194.5 54.7 %all_to_all.16 = bf16[16,128,448]{1,2,0:T(8,128)(2,1)} all-to-all(bf16[16,128,448]{1,2,0:T(8,128)(2,1)} %fusion.24), channel_id=1, replica_groups=mesh['expert'=16,'hidden'=16] {'hidden'}, dimensions={0} | all-to-all | bytes 3670016 | tf_op jit(solution)/shard_map/all_to_all | solution.py:27
  249.2 37.1 %all-gather.5.cloned.1.call-done = bf16[640,2048]{1,0:T(8,128)(2,1)} async-done(((bf16[640,128]{1,0:T(8,128)(2,1)}), bf16[640,2048]{1,0:T(8,128)(2,1)}) %all-gather.5.cloned.1.call-update) | async-done | bytes 2621456 | tf_op jit(solution)/shard_map/all_gather | solution.py:42
  286.3 3.9 %fusion.7 = bf16[640,448]{0,1:T(8,128)(2,1)S(1)} fusion(bf16[640,2048]{1,0:T(8,128)(2,1)} %all-gather.5.cloned.1.call-done, bf16[16,128,448]{1,2,0:T(8,128)(2,1)} %all_to_all.16), kind=kOutput, calls=%fused_computation.7 | convolution fusion | flops 1174691840 | bytes 5029888 | tf_op jit(solution)/shard_map/dot_general | solution.py:43
  290.2 1.1 copy.30
  291.3 8.3 %all-to-all-start.2 = ((bf16[16,40,448]{2,1,0:T(8,128)(2,1)}), bf16[16,40,448]{2,1,0:T(8,128)(2,1)S(1)}, u32[]{:S(2)}, u32[]{:S(2)}) async-start(bf16[16,40,448]{2,1,0:T(8,128)(2,1)} %bitcast.24), calls=%async_computation.2 | async-start | bytes 1310720 | tf_op jit(solution)/shard_map/all_to_all | solution.py:46
  299.6 11.2 %all-to-all-done.2 = bf16[16,40,448]{2,1,0:T(8,128)(2,1)S(1)} async-done(((bf16[16,40,448]{2,1,0:T(8,128)(2,1)}), bf16[16,40,448]{2,1,0:T(8,128)(2,1)S(1)}, u32[]{:S(2)}, u32[]{:S(2)}) %all-to-all-start.2) | async-done | bytes 573472 | tf_op jit(solution)/shard_map/all_to_all | solution.py:46
  311.3 1.2 fusion.11
  (19 shorter events, 1.4 us)
Async XLA Ops:
  6.5 167.1 %copy-start = (bf16[1,7168,128]{2,1,0:T(8,128)(2,1)S(1)}, bf16[1,7168,128]{2,1,0:T(8,128)(2,1)}, u32[]{:S(2)}) copy-start(bf16[1,7168,128]{2,1,0:T(8,128)(2,1)} %param.9) | copy-start | bytes 5505028
  6.5 167.1 %all-gather.3.cloned.1.call-start = ((), (), s32[]{:S(2)}) async-start(), calls=%async_computation.3 | async-start | bytes 9748480 | tf_op jit(solution)/shard_map/all_gather | solution.py:38
  29.7 256.6 %all-gather.5.cloned.1.call-start = ((), (), s32[]{:S(2)}) async-start(), calls=%async_computation.4 | async-start | bytes 2785280 | tf_op jit(solution)/shard_map/all_gather | solution.py:42
  173.6 6.3 %copy-start.2 = (bf16[640,7168]{0,1:T(8,128)(2,1)S(1)}, bf16[640,7168]{0,1:T(8,128)(2,1)}, u32[]{:S(2)}) copy-start(bf16[640,7168]{0,1:T(8,128)(2,1)} %all-gather.3.cloned.1.call-done) | copy-start | bytes 27525124
  173.6 6.7 %copy-start.3 = (bf16[1,7168,128]{2,1,0:T(8,128)(2,1)S(1)}, bf16[1,7168,128]{2,1,0:T(8,128)(2,1)}, u32[]{:S(2)}) copy-start(bf16[1,7168,128]{2,1,0:T(8,128)(2,1)} %param.10) | copy-start | bytes 5505028
  290.2 9.4 %copy-start.1 = (f32[256,2]{0,1:T(2,128)S(1)}, f32[256,2]{0,1:T(2,128)}, u32[]{:S(2)}) copy-start(f32[256,2]{0,1:T(2,128)} %param.8) | copy-start | bytes 6148
  291.3 19.5 %all-to-all-start.2 = ((bf16[16,40,448]{2,1,0:T(8,128)(2,1)}), bf16[16,40,448]{2,1,0:T(8,128)(2,1)S(1)}, u32[]{:S(2)}, u32[]{:S(2)}) async-start(bf16[16,40,448]{2,1,0:T(8,128)(2,1)} %bitcast.24), calls=%async_computation.2 | async-start | bytes 1310720 | tf_op jit(solution)/shard_map/all_to_all | solution.py:46
Sparse Core Ops, SparseCore 0:
  29.8 143.7 all-gather.2
  183.7 102.5 all-gather.4

commit v2 on v0

--- a/solution.py
+++ b/solution.py
@@ -30,7 +30,10 @@
     arrived = lax.all_to_all(
         leaving.reshape(experts, capacity, width), "expert", split_axis=0, concat_axis=0, tiled=True
     ).reshape(slot_count, width)
-    rows = lax.all_gather(arrived, "hidden", axis=1, tiled=True)
+    size = lax.axis_size("hidden")
+    blocks = jnp.stack([arrived for _ in range(size)])
+    blocks = lax.all_to_all(blocks, "hidden", split_axis=0, concat_axis=0)
+    rows = jnp.concatenate(blocks, axis=1)
     gate_sum = jnp.dot(rows, w_gate[0], preferred_element_type=jnp.float32)
     up_sum = jnp.dot(rows, w_up[0], preferred_element_type=jnp.float32)
     hidden = (jax.nn.silu(gate_sum) * up_sum).astype(jnp.bfloat16)

time: 320 us -> 383 us (1.20)
  blocking collectives: 74.9 us -> 287 us
  waiting for transfers between devices: 198 us -> 53.5 us
    all_to_all x0 -> x1, blocking collectives: none -> 214 us  [on_device(): blocks = lax.all_to_all(blocks, 'hidden', split_axis=0, concat_axis=0)]
    all_gather x1 -> x0, waiting for transfers between devices: 144 us -> none  [on_device(): rows = lax.all_gather(arrived, 'hidden', axis=1, tiled=True)]
  transfers between devices with their start and end apart: 3 -> 2, of which waited for: 3 -> 2; matrix products, arithmetic and copies ran while one was open for 1% -> 1% of each run, Pallas kernels for 0% -> 0%
where the time goes in v2:
time: 383 us
  blocking collectives  287 us (75%)
  waiting for transfers between devices  53.5 us (14%)
  between operations  13.5 us (4%)
  matrix products  13.1 us (3%)
  starting transfers between devices  8.26 us (2%)
  local copies, waits for them, and re-layouts  6.65 us (2%)
    all_to_all x1, blocking collectives, on_device(): blocks = lax.all_to_all(blocks, 'hidden', split_axis=0, concat_axis=0)  214 us
    all_to_all x1, blocking collectives, on_device(): lax.all_to_all(w_down[0], 'hidden', split_axis=1, concat_axis=0, tiled=True)  54.5 us
    all_gather x1, waiting for transfers between devices, on_device(): every_hidden = lax.all_gather(hidden, 'hidden', axis=1, tiled=True)  42.3 us
    all_to_all x1, blocking collectives, on_device(): lax.all_to_all(leaving.reshape(experts, capacity, width), 'expert', split...  18.5 us
    all_to_all x1, waiting for transfers between devices, on_device(): lax.all_to_all(produced.reshape(experts, capacity, width), 'expert', spli...  11.2 us
    all_to_all x1, starting transfers between devices, on_device(): lax.all_to_all(produced.reshape(experts, capacity, width), 'expert', spli...  8.26 us
  transfers between devices with their start and end apart: 2, of which 2 were waited for; matrix products, arithmetic and copies ran while one was open for 1% of the time, Pallas kernels for 0%

profile of v2, /device:TPU:1, one launch (start us, length us, event | category | flops | bytes accessed | tf_op | source)
XLA Modules:
  0.0 383.0 jit_solution(216109219206178962)
XLA Ops:
  6.5 0.0 copy-start
  6.5 0.0 all-gather.2.cloned.1.call-start
  6.5 0.8 fusion.24
  7.4 0.2 convolution_add_fusion
  7.5 0.7 select_reduce_fusion
  8.3 1.5 convolution_convert_fusion
  9.8 0.3 copy.17
  10.1 18.5 %all_to_all.34 = bf16[16,40,448]{2,1,0:T(8,128)(2,1)S(1)} all-to-all(bf16[16,40,448]{2,1,0:T(8,128)(2,1)S(1)} %bitcast.44), channel_id=1, replica_groups=mesh['expert'=16,'hidden'=16] {'expert'}, dimensions={0} | all-to-all | bytes 1146880 | tf_op jit(solution)/shard_map/all_to_all | solution.py:30
  28.5 0.3 copy.18
  28.8 1.1 stack.3
  29.9 213.5 %all_to_all.35 = bf16[16,640,448]{1,2,0:T(8,128)(2,1)S(1)} all-to-all(bf16[16,640,448]{1,2,0:T(8,128)(2,1)S(1)} %stack.3), channel_id=1, replica_groups=mesh['expert'=16,'hidden'=16] {'hidden'}, dimensions={0} | all-to-all | bytes 18350080 | tf_op jit(solution)/shard_map/all_to_all | solution.py:35
  243.4 0.0 copy-done
  243.4 0.0 copy-start.2
  243.4 2.6 fusion.5
  246.0 0.0 copy-done.2
  246.0 3.2 fusion.15
  249.3 0.0 all-gather.2.cloned.1.call-update
  249.3 3.9 %copy.19 = bf16[1,128,7168]{1,2,0:T(8,128)(2,1)} copy(bf16[1,128,7168]{2,1,0:T(8,128)(2,1)} %param.11) | data formatting | bytes 3670016 | tf_op args[5]
  253.2 54.5 %all_to_all.36 = bf16[128,16,448]{0,2,1:T(8,128)(2,1)} all-to-all(bf16[128,16,448]{0,2,1:T(8,128)(2,1)} %bitcast.41), channel_id=1, replica_groups=mesh['expert'=16,'hidden'=16] {'hidden'}, dimensions={1} | all-to-all | bytes 3670016 | tf_op jit(solution)/shard_map/all_to_all | solution.py:26
  307.7 42.3 %all-gather.2.cloned.1.call-done = bf16[640,2048]{1,0:T(8,128)(2,1)} async-done(((bf16[640,128]{1,0:T(8,128)(2,1)}), bf16[640,2048]{1,0:T(8,128)(2,1)}) %all-gather.2.cloned.1.call-update) | async-done | bytes 2621456 | tf_op jit(solution)/shard_map/all_gather | solution.py:40
  350.0 3.9 %fusion.7 = bf16[640,448]{0,1:T(8,128)(2,1)S(1)} fusion(bf16[640,2048]{1,0:T(8,128)(2,1)} %all-gather.2.cloned.1.call-done, bf16[128,16,448]{0,2,1:T(8,128)(2,1)} %all_to_all.36), kind=kOutput, calls=%fused_computation.7 | convolution fusion | flops 1174691840 | bytes 5029888 | tf_op jit(solution)/shard_map/dot_general | solution.py:41
  353.9 0.0 copy-start.1
  353.9 1.1 copy.21
  355.0 8.3 %all-to-all-start.3 = ((bf16[16,40,448]{2,1,0:T(8,128)(2,1)}), bf16[16,40,448]{2,1,0:T(8,128)(2,1)S(1)}, u32[]{:S(2)}, u32[]{:S(2)}) async-start(bf16[16,40,448]{2,1,0:T(8,128)(2,1)} %bitcast.12), calls=%async_computation.3 | async-start | bytes 1310720 | tf_op jit(solution)/shard_map/all_to_all | solution.py:44
  363.3 0.0 copy-done.1
  363.3 11.2 %all-to-all-done.3 = bf16[16,40,448]{2,1,0:T(8,128)(2,1)S(1)} async-done(((bf16[16,40,448]{2,1,0:T(8,128)(2,1)}), bf16[16,40,448]{2,1,0:T(8,128)(2,1)S(1)}, u32[]{:S(2)}, u32[]{:S(2)}) %all-to-all-start.3) | async-done | bytes 573472 | tf_op jit(solution)/shard_map/all_to_all | solution.py:44
  374.5 0.5 convolution_multiply_fusion.1
  375.0 1.2 fusion.11
  (4 shorter events, 0.0 us)
Async XLA Ops:
  6.5 236.9 %copy-start = (bf16[1,7168,128]{2,1,0:T(8,128)(2,1)S(1)}, bf16[1,7168,128]{2,1,0:T(8,128)(2,1)}, u32[]{:S(2)}) copy-start(bf16[1,7168,128]{2,1,0:T(8,128)(2,1)} %param.9) | copy-start | bytes 5505028
  6.5 343.5 %all-gather.2.cloned.1.call-start = ((), (), s32[]{:S(2)}) async-start(), calls=%async_computation.4 | async-start | bytes 2785280 | tf_op jit(solution)/shard_map/all_gather | solution.py:40
  243.4 2.6 copy-start.2
  353.9 9.4 %copy-start.1 = (f32[256,2]{0,1:T(2,128)S(1)}, f32[256,2]{0,1:T(2,128)}, u32[]{:S(2)}) copy-start(f32[256,2]{0,1:T(2,128)} %param.8) | copy-start | bytes 6148
  355.0 19.5 %all-to-all-start.3 = ((bf16[16,40,448]{2,1,0:T(8,128)(2,1)}), bf16[16,40,448]{2,1,0:T(8,128)(2,1)S(1)}, u32[]{:S(2)}, u32[]{:S(2)}) async-start(bf16[16,40,448]{2,1,0:T(8,128)(2,1)} %bitcast.12), calls=%async_computation.3 | async-start | bytes 1310720 | tf_op jit(solution)/shard_map/all_to_all | solution.py:44
Sparse Core Ops, SparseCore 0:
  249.4 100.5 all-gather.1
